TPU v7x, 32 devices: a whole 2x2x4 slice. The times are simulated.
32 devices in a mesh: groups: 2 (over y), mz: 4 (over z), pix: 4 (over x, core).
Axes of the slice: x: 2, y: 2, z: 4, core: 2. Of those that a mesh axis runs over, the one named last changes fastest.
Arguments:
- spectra: bfloat16 [1024, 262144], P(('groups', 'pix'), 'mz'), parts along dimension 0
- kernel: bfloat16 [129], replicated, may hold values from 0.0009994507 to 0.029907227
- probes: bfloat16 [262144, 128], P('mz'), may hold values from -0.01171875 to 0.01171875
Outputs:
- basis: bfloat16 [1024, 128], P(('groups', 'pix')), parts along dimension 0
- projected: bfloat16 [256, 262144], P(('groups', 'pix'), 'mz'), parts along dimension 0
There are 2 independent parts, one for each index of `groups`. A program takes and returns all parts, laid end to end along the dimension named above; an argument that names none is the same for every part. Nothing has to cross between parts.
All inputs are finite; a program needn't handle non-finite values.
Results may differ from a plain program's by a relative error of at most 0.019.
Values may be sent and summed in bfloat16 or wider, within the bound.
A program may use at most 192 MiB of HBM per device.

v0:
```python
import functools
import math

import jax
import jax.numpy as jnp
from jax import lax
from jax.experimental import pallas as pl
from jax.experimental.pallas import tpu as pltpu
from jax.sharding import PartitionSpec as P

LANES = 128
OUT = 256
WIN = OUT + 2 * LANES


MESH = pl.DeviceIdType.MESH
HIGHEST = lax.Precision.HIGHEST
PANEL = 8
EARLY = 3
AHEAD = 2


def whiten(a_ref, x_ref):
    size = a_ref.shape[0]
    row = lax.broadcasted_iota(jnp.int32, (PANEL, 1), 0)
    a = a_ref[...]
    x = (
        lax.broadcasted_iota(jnp.int32, (size, size), 0)
        == lax.broadcasted_iota(jnp.int32, (size, size), 1)
    ).astype(jnp.float32)
    blocks = size // PANEL
    a = [a[i * PANEL : (i + 1) * PANEL] for i in range(blocks)]
    x = [x[i * PANEL : (i + 1) * PANEL] for i in range(blocks)]
    for index in range(blocks):
        p, q = a[index], x[index]
        rows_p, rows_q = [], []
        spread = [
            jnp.broadcast_to(p[:, index * PANEL + t : index * PANEL + t + 1], p.shape)
            for t in range(PANEL)
        ]
        for t in range(PANEL):
            inv = lax.rsqrt(spread[t][t : t + 1])
            r, y = p[t : t + 1] * inv, q[t : t + 1] * inv
            rows_p.append(r)
            rows_q.append(y)
            if t + 1 < PANEL:
                scale = jnp.where(row > t, spread[t] * inv, 0.0)
                p = p - scale * r
                q = q - scale * y
                for j in range(t + 1, PANEL):
                    spread[j] = spread[j] - scale * (spread[j][t : t + 1] * inv)
        x_ref[index * PANEL : (index + 1) * PANEL, :] = jnp.concatenate(rows_q, axis=0)
        if index + 1 < blocks:
            turned = jnp.concatenate(rows_p, axis=0).T
            for later in range(index + 1, blocks):
                for t in range(PANEL):
                    scale = turned[later * PANEL : (later + 1) * PANEL, t : t + 1]
                    a[later] = a[later] - scale * rows_p[t]
                    x[later] = x[later] - scale * rows_q[t]


def fused_kernel(
    n_mz, n_pix, factor, pixels, early, ahead, spectra, u_ref, probes, basis, out,
    raw, tap, w_ref, halo, cleaned, total, parts, parts_in, sketch, gram, gram_in, x_ref,
    lhs, give, core_in, hold, x_give, x_in, acc, out_v, lhs_far, early_in, sketch_far,
    raw_sem, tap_sem, halo_send, halo_recv, parts_send, parts_recv, all_send, all_recv,
    gram_send, gram_recv, give_sem, core_sem, x_send_sem, x_recv_sem, store_sem,
    early_send, early_recv, far_send, far_recv,
):
    bins = spectra.shape[1]
    slots, tile = tap.shape[0], tap.shape[1]
    tiles = bins // tile
    chips = n_pix // 2
    share = lhs.shape[0] // n_pix
    half = chips * share
    chunks, width = acc.shape[0], acc.shape[2]
    per = tile // width
    ring = give.shape[0]
    groups, mz, pix = lax.axis_index("groups"), lax.axis_index("mz"), lax.axis_index("pix")
    core = lax.rem(pix, 2)
    chip = lax.div(pix, 2)
    other = 1 - core

    def at_z(d):
        return (groups, lax.rem(mz + d, n_mz), pix)

    def at_pix(d):
        return (groups, mz, lax.rem(pix + d, n_pix))

    def device(at_chip, at_core):
        return (groups, mz, at_chip * 2 + at_core)

    def chip_of(d):
        return lax.rem(chip + d, chips)

    def tile_of(pos):
        return jnp.where(pos == tiles - 1, tiles - 1, jnp.where(pos == tiles - 2, 0, pos + 1))

    def each_load(pos, act):
        slot = lax.rem(pos, slots)

        @pl.when(pos < tiles - 2)
        def _():
            begin = pl.multiple_of((pos + 1) * tile - LANES, LANES)
            act(pltpu.make_async_copy(
                spectra.at[:, pl.ds(begin, tile + 2 * LANES)], raw.at[slot], raw_sem.at[slot]))

        @pl.when(pos == tiles - 2)
        def _():
            act(pltpu.make_async_copy(
                spectra.at[:, pl.ds(0, tile + LANES)],
                raw.at[slot, :, pl.ds(LANES, tile + LANES)], raw_sem.at[slot]))

        @pl.when(pos == tiles - 1)
        def _():
            act(pltpu.make_async_copy(
                spectra.at[:, pl.ds(bins - tile - LANES, tile + LANES)],
                raw.at[slot, :, pl.ds(0, tile + LANES)], raw_sem.at[slot]))

        begin = pl.multiple_of(tile_of(pos) * tile, tile)
        act(pltpu.make_async_copy(probes.at[pl.ds(begin, tile), :], tap.at[slot], tap_sem.at[slot]))

    both = chunks - 2 * early

    def whole_of(e, at_chip):
        return per + 2 * e + at_chip

    def chunk_of(i):
        return jnp.where(i < per, i, jnp.where(
            i < both, i + 2 * early, whole_of(i - both, chip)))

    def send_early(e):
        return pltpu.make_async_remote_copy(
            src_ref=cleaned.at[whole_of(e, 1 - chip)], dst_ref=early_in.at[e],
            send_sem=early_send.at[e], recv_sem=early_recv.at[e],
            device_id=device(1 - chip, core), device_id_type=MESH,
        )

    for pos in range(min(slots, tiles)):
        each_load(jnp.int32(pos), lambda c: c.start())

    barrier = pltpu.get_barrier_semaphore()
    for d in range(1, n_mz):
        pl.semaphore_signal(barrier, inc=1, device_id=at_z(d), device_id_type=MESH)
    for d in range(1, n_pix):
        pl.semaphore_signal(barrier, inc=1, device_id=at_pix(d), device_id_type=MESH)

    base = jnp.broadcast_to(u_ref[...], (WIN, WIN))
    w_ref[...] = pltpu.roll(base, 0, 1, stride=1, stride_axis=0)[:, :OUT].astype(jnp.bfloat16)
    total[...] = jnp.zeros_like(total)

    pl.semaphore_wait(barrier, n_mz - 1 + n_pix - 1)

    to_right = pltpu.make_async_remote_copy(
        src_ref=spectra.at[:, pl.ds(bins - LANES, LANES)], dst_ref=halo.at[0],
        send_sem=halo_send.at[0], recv_sem=halo_recv.at[0],
        device_id=at_z(1), device_id_type=MESH,
    )
    to_left = pltpu.make_async_remote_copy(
        src_ref=spectra.at[:, pl.ds(0, LANES)], dst_ref=halo.at[1],
        send_sem=halo_send.at[1], recv_sem=halo_recv.at[1],
        device_id=at_z(n_mz - 1), device_id_type=MESH,
    )

    @pl.when(mz < n_mz - 1)
    def _():
        to_right.start()

    @pl.when(mz > 0)
    def _():
        to_left.start()

    @pl.when(mz == 0)
    def _():
        halo[0] = jnp.zeros(halo.shape[1:], halo.dtype)

    @pl.when(mz == n_mz - 1)
    def _():
        halo[1] = jnp.zeros(halo.shape[1:], halo.dtype)

    def clean(pos):
        slot = lax.rem(pos, slots)
        at = tile_of(pos)
        each_load(pos, lambda c: c.wait())

        @pl.when(pos == tiles - 2)
        def _():
            @pl.when(mz > 0)
            def _():
                to_right.wait_recv()

            raw[slot, :, :LANES] = halo[0]

        @pl.when(pos == tiles - 1)
        def _():
            @pl.when(mz < n_mz - 1)
            def _():
                to_left.wait_recv()

            raw[slot, :, tile + LANES :] = halo[1]

        w = w_ref[...]
        done = []
        for j in range(tile // OUT):
            window = raw[slot, :, j * OUT : j * OUT + WIN]
            smooth = jnp.dot(window, w, preferred_element_type=jnp.float32)
            mine = raw[slot, :, LANES + j * OUT : LANES + (j + 1) * OUT].astype(jnp.float32)
            one = (mine - smooth).astype(jnp.bfloat16)
            piece, inside = (j * OUT) // width, (j * OUT) % width
            cleaned[at * per + piece, :, inside : inside + OUT] = one
            done.append(one)
        total[...] += jnp.dot(
            jnp.concatenate(done, axis=1), tap[slot], preferred_element_type=jnp.float32
        )

    @pl.loop(0, tiles)
    def _(pos):
        clean(pos)

        @pl.when(pos + slots < tiles)
        def _():
            each_load(pos + slots, lambda c: c.start())

        if ahead:
            @pl.when(pos < ahead)
            def _():
                send_early(pos).start()

    @pl.when(mz < n_mz - 1)
    def _():
        to_right.wait_send()

    @pl.when(mz > 0)
    def _():
        to_left.wait_send()

    rows = parts.shape[1]
    for z in range(n_mz):
        parts[z] = total[z * rows : (z + 1) * rows]

    def scatter(d):
        return pltpu.make_async_remote_copy(
            src_ref=parts.at[lax.rem(mz + d, n_mz)], dst_ref=parts_in.at[d - 1],
            send_sem=parts_send.at[d - 1], recv_sem=parts_recv.at[d - 1],
            device_id=at_z(d), device_id_type=MESH,
        )

    for d in range(1, n_mz):
        scatter(d).start()
    mine = parts[mz]
    for d in range(1, n_mz):
        scatter(d).wait_recv()
        mine = mine + parts_in[d - 1]
    sketch[mz] = mine

    def gather(d, owner):
        return pltpu.make_async_remote_copy(
            src_ref=sketch.at[mz], dst_ref=sketch.at[owner],
            send_sem=all_send.at[d - 1], recv_sem=all_recv.at[d - 1],
            device_id=at_z(d), device_id_type=MESH,
        )

    for d in range(1, n_mz):
        gather(d, mz).start()
    for d in range(1, n_mz):
        gather(d, lax.rem(mz + n_mz - d, n_mz)).wait_recv()
    sk = jnp.concatenate([sketch[z] for z in range(n_mz)], axis=0)

    gram[...] = lax.dot_general(
        sk, sk, (((0,), (0,)), ((), ())), precision=HIGHEST, preferred_element_type=jnp.float32
    )

    def share_gram(d):
        return pltpu.make_async_remote_copy(
            src_ref=gram, dst_ref=gram_in.at[d - 1],
            send_sem=gram_send.at[d - 1], recv_sem=gram_recv.at[d - 1],
            device_id=at_pix(d), device_id_type=MESH,
        )

    for d in range(1, n_pix):
        share_gram(d).start()
    to_far = pltpu.make_async_remote_copy(
        src_ref=sketch, dst_ref=sketch_far, send_sem=far_send.at[0], recv_sem=far_recv.at[0],
        device_id=device(1 - chip, core), device_id_type=MESH,
    )
    if early:
        to_far.start()
    full = gram[...]
    for d in range(1, n_pix):
        share_gram(d).wait_recv()
        full = full + gram_in[d - 1]
    if early:
        to_far.wait_recv()
        for e in range(ahead, early):
            send_early(e).start()
    total[...] = full * (1.0 / pixels)
    whiten(total, x_ref)
    x = x_ref[...]
    by_lane = (((1,), (1,)), ((), ()))

    def fill(target, of):
        flipped = lax.dot_general(
            x, of, by_lane, precision=HIGHEST, preferred_element_type=jnp.float32
        ).astype(jnp.bfloat16)
        basis_t = flipped.reshape(n_pix, share, flipped.shape[1])
        for chunk in range(n_pix):
            d = lax.rem(chunk // 2 - chip + chips, chips)
            at = d * share + jnp.where(core == chunk % 2, half, 0)
            target[pl.ds(pl.multiple_of(at, share), share), :] = basis_t[chunk]

    fill(lhs, sk)

    def to_core(k):
        return pltpu.make_async_remote_copy(
            src_ref=give.at[lax.rem(k, ring)], dst_ref=core_in.at[k],
            send_sem=give_sem.at[lax.rem(k, ring)], recv_sem=core_sem.at[k],
            device_id=device(chip, other), device_id_type=MESH,
        )

    def to_chip(d, k):
        return pltpu.make_async_remote_copy(
            src_ref=x_give.at[d - 1, k], dst_ref=x_in.at[d - 1, k],
            send_sem=x_send_sem.at[d - 1, k], recv_sem=x_recv_sem.at[d - 1, k],
            device_id=device(chip_of(d), core), device_id_type=MESH,
        )

    def product(left, right):
        part = jnp.dot(left, right, preferred_element_type=jnp.float32) * factor
        return part.astype(jnp.bfloat16)

    def first(i, alone):
        slot = lax.rem(i, ring)

        @pl.when(i >= ring)
        def _():
            to_core(i - ring).wait_send()

        part = product(lhs[...], cleaned[chunk_of(i)])
        if alone:
            send_early(i - both).wait_recv()
            far = product(lhs_far[...], early_in[i - both])
            part = (part.astype(jnp.float32) + far.astype(jnp.float32)).astype(jnp.bfloat16)
        give[slot] = part[:half]
        to_core(i).start()
        hold[slot] = part[half:]

    def second(i):
        to_core(i).wait_recv()
        slot = lax.rem(i, ring)
        k = chunk_of(i)
        added = hold[slot].astype(jnp.float32) + core_in[i].astype(jnp.float32)
        acc[k] = added[:share]
        for d in range(1, chips):
            x_give[d - 1, k] = added[d * share : (d + 1) * share].astype(jnp.bfloat16)
            to_chip(d, k).start()

    def store(n, k):
        slot = lax.rem(n, ring)
        return pltpu.make_async_copy(
            out_v.at[slot], out.at[:, pl.ds(pl.multiple_of(k * width, width), width)],
            store_sem.at[slot],
        )

    def emit(n, k, value):
        @pl.when(n >= ring)
        def _():
            store(n - ring, k).wait()

        out_v[lax.rem(n, ring)] = value.astype(jnp.bfloat16)
        store(n, k).start()

    lag = min(ring - 1, both)
    mine = chunks - early

    @pl.loop(0, lag)
    def _(i):
        first(i, False)

    basis[...] = lax.dot_general(
        sk, x, by_lane, precision=HIGHEST, preferred_element_type=jnp.float32
    ).astype(jnp.bfloat16)

    @pl.loop(lag, both)
    def _(i):
        first(i, False)
        second(i - lag)

    if early:
        fill(lhs_far, jnp.concatenate([sketch_far[z] for z in range(n_mz)], axis=0))

        @pl.loop(both, mine)
        def _(i):
            first(i, True)
            second(i - lag)

    @pl.loop(mine - lag, mine)
    def _(i):
        second(i)

    @pl.loop(max(mine - ring, 0), mine)
    def _(i):
        to_core(i).wait_send()

    for d in range(1, n_mz):
        scatter(d).wait_send()
        gather(d, mz).wait_send()
    for d in range(1, n_pix):
        share_gram(d).wait_send()
    if early:
        to_far.wait_send()
        for e in range(early):
            send_early(e).wait_send()

        @pl.loop(0, early)
        def _(e):
            emit(e, whole_of(e, chip), acc[whole_of(e, chip)])

    @pl.loop(0, both)
    def _(i):
        k = chunk_of(i)
        added = acc[k]
        for d in range(1, chips):
            to_chip(d, k).wait()
            added = added + x_in[d - 1, k].astype(jnp.float32)
        emit(early + i, k, added)

    if early:
        @pl.loop(0, early)
        def _(e):
            k = whole_of(e, 1 - chip)
            to_chip(1, k).wait_recv()
            emit(early + both + e, k, x_in[0, k])
            to_chip(1, whole_of(e, chip)).wait_send()

    @pl.loop(max(chunks - ring, 0), chunks)
    def _(n):
        store(n, n).wait()


def per_device(spectra, kernel, probes):
    rows, bins = spectra.shape
    cols = probes.shape[1]
    n_pix, n_mz = lax.axis_size("pix"), lax.axis_size("mz")
    pixels = rows * n_pix
    factor = 1.0 / math.sqrt(float(pixels))
    taps = kernel.shape[0]
    low = WIN - (LANES - taps // 2) - (taps - 1)
    u = jnp.pad(kernel[::-1].astype(jnp.float32), (low, WIN - low - taps))[None, :]
    share = cols // n_pix
    chips = n_pix // 2
    half = chips * share
    tile = min(4096, bins // 2)
    width = min(2048, tile)
    chunks = bins // width
    slots, ring = 3, 4
    fits = chips == 2 and tile == 2 * width and bins // tile >= 8
    early, ahead = (EARLY, AHEAD) if fits else (0, 0)
    kept = max(early, 1)
    away = max(chips - 1, 1)
    part = rows // n_mz
    bf16, f32 = jnp.bfloat16, jnp.float32
    dma = pltpu.SemaphoreType.DMA
    return pl.pallas_call(
        functools.partial(fused_kernel, n_mz, n_pix, factor, float(pixels), early, ahead),
        in_specs=[
            pl.BlockSpec(memory_space=pl.ANY),
            pl.BlockSpec(memory_space=pltpu.VMEM),
            pl.BlockSpec(memory_space=pl.ANY),
        ],
        out_specs=[pl.BlockSpec(memory_space=pltpu.VMEM), pl.BlockSpec(memory_space=pl.ANY)],
        out_shape=[
            jax.ShapeDtypeStruct((rows, cols), bf16),
            jax.ShapeDtypeStruct((share, bins), bf16),
        ],
        scratch_shapes=[
            pltpu.VMEM((slots, rows, tile + 2 * LANES), bf16),
            pltpu.VMEM((slots, tile, cols), bf16),
            pltpu.VMEM((WIN, OUT), bf16),
            pltpu.VMEM((2, rows, LANES), bf16),
            pltpu.VMEM((chunks, rows, width), bf16),
            pltpu.VMEM((rows, cols), f32),
            pltpu.VMEM((n_mz, part, cols), f32),
            pltpu.VMEM((n_mz - 1, part, cols), f32),
            pltpu.VMEM((n_mz, part, cols), f32),
            pltpu.VMEM((cols, cols), f32),
            pltpu.VMEM((n_pix - 1, cols, cols), f32),
            pltpu.VMEM((cols, cols), f32),
            pltpu.VMEM((cols, rows), bf16),
            pltpu.VMEM((ring, half, width), bf16),
            pltpu.VMEM((chunks, half, width), bf16),
            pltpu.VMEM((ring, half, width), bf16),
            pltpu.VMEM((away, chunks, share, width), bf16),
            pltpu.VMEM((away, chunks, share, width), bf16),
            pltpu.VMEM((chunks, share, width), f32),
            pltpu.VMEM((ring, share, width), bf16),
            pltpu.VMEM((cols, rows), bf16),
            pltpu.VMEM((kept, rows, width), bf16),
            pltpu.VMEM((n_mz, part, cols), f32),
            dma((slots,)),
            dma((slots,)),
            dma((2,)),
            dma((2,)),
            dma((n_mz - 1,)),
            dma((n_mz - 1,)),
            dma((n_mz - 1,)),
            dma((n_mz - 1,)),
            dma((n_pix - 1,)),
            dma((n_pix - 1,)),
            dma((ring,)),
            dma((chunks,)),
            dma((away, chunks)),
            dma((away, chunks)),
            dma((ring,)),
            dma((kept,)),
            dma((kept,)),
            dma((1,)),
            dma((1,)),
        ],
        compiler_params=pltpu.CompilerParams(
            collective_id=0, has_side_effects=True, vmem_limit_bytes=58 * 2**20
        ),
        cost_estimate=pl.CostEstimate(
            flops=2 * rows * bins * (WIN + 2 * cols),
            bytes_accessed=2 * bins * (rows + cols + share),
            transcendentals=0,
        ),
    )(spectra, u, probes)


def solution(mesh):
    in_specs = (P(("groups", "pix"), "mz"), P(), P("mz", None))
    out_specs = (P(("groups", "pix"), None), P(("groups", "pix"), "mz"))
    return jax.shard_map(
        per_device, mesh=mesh, in_specs=in_specs, out_specs=out_specs, check_vma=False
    )
```

profile of v0, /device:TPU:0, one launch (start us, length us, event | category | flops | bytes accessed | tf_op | source)
XLA Modules:
  0.0 139.1 jit_solution(51076138247357888)
XLA Ops:
  0.6 0.7 reverse
  1.4 0.1 slice
  1.5 0.7 pad_convert_fusion
  2.1 131.1 %shard_map.50 = (bf16[128,128]{1,0:T(8,128)(2,1)}, bf16[32,65536]{1,0:T(8,128)(2,1)}) custom-call(bf16[128,65536]{1,0:T(8,128)(2,1)} %spectra.1, f32[1,512]{1,0:T(1,128)} %bitcast.2, bf16[65536,128]{1,0:T(8,128)(2,1)} %probes.1), custom_call_target="tpu_custom_call" | custom-call | flops 12884901888 | bytes 37748736 | tf_op jit(solution)/shard_map/pallas_call | solution.py:463
  133.2 1.4 copy.7
  134.6 4.5 %copy.8 = bf16[32,65536]{1,0:T(8,128)(2,1)} copy(bf16[32,65536]{1,0:T(8,128)(2,1)} %get-tuple-element.5) | data formatting | bytes 8388608
where the time goes:
time: 139 us
  Pallas kernels  131 us (94%)
  local copies, waits for them, and re-layouts  6.67 us (5%)
    pallas_call x1, Pallas kernels, per_device(): pl.pallas_call(functools.partial(fused_kernel, n_mz, n_pix, factor, float...  131 us
    unnamed x4, local copies, waits for them, and re-layouts  6.67 us

commit v1 on v0

--- a/solution.py
+++ b/solution.py
@@ -16,8 +16,9 @@
 MESH = pl.DeviceIdType.MESH
 HIGHEST = lax.Precision.HIGHEST
 PANEL = 8
-EARLY = 3
-AHEAD = 2
+EARLY = 5
+AHEAD = 4
+MET = 4
 
 
 def whiten(a_ref, x_ref):
@@ -60,11 +61,11 @@
 
 
 def fused_kernel(
-    n_mz, n_pix, factor, pixels, early, ahead, spectra, u_ref, probes, basis, out,
-    raw, tap, w_ref, halo, cleaned, total, parts, parts_in, sketch, gram, gram_in, x_ref,
-    lhs, give, core_in, hold, x_give, x_in, acc, out_v, lhs_far, early_in, sketch_far,
+    n_mz, n_pix, factor, pixels, early, ahead, spectra, k_ref, probes, basis, out,
+    raw, tap, line, w_ref, halo, cleaned, total, parts, parts_in, sketch, gram, gram_in, x_ref,
+    lhs, give, core_in, hold, x_give, x_in, acc, lhs_far, early_in, sketch_far,
     raw_sem, tap_sem, halo_send, halo_recv, parts_send, parts_recv, all_send, all_recv,
-    gram_send, gram_recv, give_sem, core_sem, x_send_sem, x_recv_sem, store_sem,
+    gram_send, gram_recv, give_sem, core_sem, x_send_sem, x_recv_sem,
     early_send, early_recv, far_send, far_recv,
 ):
     bins = spectra.shape[1]
@@ -121,6 +122,7 @@
         act(pltpu.make_async_copy(probes.at[pl.ds(begin, tile), :], tap.at[slot], tap_sem.at[slot]))
 
     both = chunks - 2 * early
+    met = min(MET, tiles - 2)
 
     def whole_of(e, at_chip):
         return per + 2 * e + at_chip
@@ -145,11 +147,13 @@
     for d in range(1, n_pix):
         pl.semaphore_signal(barrier, inc=1, device_id=at_pix(d), device_id_type=MESH)
 
-    base = jnp.broadcast_to(u_ref[...], (WIN, WIN))
-    w_ref[...] = pltpu.roll(base, 0, 1, stride=1, stride_axis=0)[:, :OUT].astype(jnp.bfloat16)
+    taps = k_ref.shape[0]
+    line[...] = jnp.zeros_like(line)
+    line[:, :taps] = k_ref[...].astype(jnp.float32).reshape(1, taps)
+    base = jnp.broadcast_to(line[...], (OUT, WIN))
+    band = pltpu.roll(base, LANES - taps // 2, 1, stride=1, stride_axis=0)
+    w_ref[...] = band.T.astype(jnp.bfloat16)
     total[...] = jnp.zeros_like(total)
-
-    pl.semaphore_wait(barrier, n_mz - 1 + n_pix - 1)
 
     to_right = pltpu.make_async_remote_copy(
         src_ref=spectra.at[:, pl.ds(bins - LANES, LANES)], dst_ref=halo.at[0],
@@ -161,14 +165,6 @@
         send_sem=halo_send.at[1], recv_sem=halo_recv.at[1],
         device_id=at_z(n_mz - 1), device_id_type=MESH,
     )
-
-    @pl.when(mz < n_mz - 1)
-    def _():
-        to_right.start()
-
-    @pl.when(mz > 0)
-    def _():
-        to_left.start()
 
     @pl.when(mz == 0)
     def _():
@@ -215,16 +211,26 @@
 
     @pl.loop(0, tiles)
     def _(pos):
+        @pl.when(pos == met)
+        def _():
+            pl.semaphore_wait(barrier, n_mz - 1 + n_pix - 1)
+
+            @pl.when(mz < n_mz - 1)
+            def _():
+                to_right.start()
+
+            @pl.when(mz > 0)
+            def _():
+                to_left.start()
+
+            for e in range(ahead):
+                send_early(e).start()
+
         clean(pos)
 
         @pl.when(pos + slots < tiles)
         def _():
             each_load(pos + slots, lambda c: c.start())
-
-        if ahead:
-            @pl.when(pos < ahead)
-            def _():
-                send_early(pos).start()
 
     @pl.when(mz < n_mz - 1)
     def _():
@@ -354,20 +360,8 @@
             x_give[d - 1, k] = added[d * share : (d + 1) * share].astype(jnp.bfloat16)
             to_chip(d, k).start()
 
-    def store(n, k):
-        slot = lax.rem(n, ring)
-        return pltpu.make_async_copy(
-            out_v.at[slot], out.at[:, pl.ds(pl.multiple_of(k * width, width), width)],
-            store_sem.at[slot],
-        )
-
-    def emit(n, k, value):
-        @pl.when(n >= ring)
-        def _():
-            store(n - ring, k).wait()
-
-        out_v[lax.rem(n, ring)] = value.astype(jnp.bfloat16)
-        store(n, k).start()
+    def emit(k, value):
+        out[:, pl.ds(pl.multiple_of(k * width, width), width)] = value.astype(jnp.bfloat16)
 
     lag = min(ring - 1, both)
     mine = chunks - early
@@ -413,7 +407,7 @@
 
         @pl.loop(0, early)
         def _(e):
-            emit(e, whole_of(e, chip), acc[whole_of(e, chip)])
+            emit(whole_of(e, chip), acc[whole_of(e, chip)])
 
     @pl.loop(0, both)
     def _(i):
@@ -422,19 +416,15 @@
         for d in range(1, chips):
             to_chip(d, k).wait()
             added = added + x_in[d - 1, k].astype(jnp.float32)
-        emit(early + i, k, added)
+        emit(k, added)
 
     if early:
         @pl.loop(0, early)
         def _(e):
             k = whole_of(e, 1 - chip)
             to_chip(1, k).wait_recv()
-            emit(early + both + e, k, x_in[0, k])
+            emit(k, x_in[0, k])
             to_chip(1, whole_of(e, chip)).wait_send()
-
-    @pl.loop(max(chunks - ring, 0), chunks)
-    def _(n):
-        store(n, n).wait()
 
 
 def per_device(spectra, kernel, probes):
@@ -443,17 +433,14 @@
     n_pix, n_mz = lax.axis_size("pix"), lax.axis_size("mz")
     pixels = rows * n_pix
     factor = 1.0 / math.sqrt(float(pixels))
-    taps = kernel.shape[0]
-    low = WIN - (LANES - taps // 2) - (taps - 1)
-    u = jnp.pad(kernel[::-1].astype(jnp.float32), (low, WIN - low - taps))[None, :]
     share = cols // n_pix
     chips = n_pix // 2
     half = chips * share
     tile = min(4096, bins // 2)
-    width = min(2048, tile)
+    width = min(1024, tile)
     chunks = bins // width
     slots, ring = 3, 4
-    fits = chips == 2 and tile == 2 * width and bins // tile >= 8
+    fits = chips == 2 and tile % width == 0 and bins // tile >= 8
     early, ahead = (EARLY, AHEAD) if fits else (0, 0)
     kept = max(early, 1)
     away = max(chips - 1, 1)
@@ -467,14 +454,15 @@
             pl.BlockSpec(memory_space=pltpu.VMEM),
             pl.BlockSpec(memory_space=pl.ANY),
         ],
-        out_specs=[pl.BlockSpec(memory_space=pltpu.VMEM), pl.BlockSpec(memory_space=pl.ANY)],
+        out_specs=[pl.BlockSpec(memory_space=pltpu.VMEM), pl.BlockSpec(memory_space=pltpu.VMEM)],
         out_shape=[
-            jax.ShapeDtypeStruct((rows, cols), bf16),
-            jax.ShapeDtypeStruct((share, bins), bf16),
+            pltpu.VMEM((rows, cols), bf16),
+            pltpu.VMEM((share, bins), bf16),
         ],
         scratch_shapes=[
             pltpu.VMEM((slots, rows, tile + 2 * LANES), bf16),
             pltpu.VMEM((slots, tile, cols), bf16),
+            pltpu.VMEM((1, WIN), f32),
             pltpu.VMEM((WIN, OUT), bf16),
             pltpu.VMEM((2, rows, LANES), bf16),
             pltpu.VMEM((chunks, rows, width), bf16),
@@ -492,7 +480,6 @@
             pltpu.VMEM((away, chunks, share, width), bf16),
             pltpu.VMEM((away, chunks, share, width), bf16),
             pltpu.VMEM((chunks, share, width), f32),
-            pltpu.VMEM((ring, share, width), bf16),
             pltpu.VMEM((cols, rows), bf16),
             pltpu.VMEM((kept, rows, width), bf16),
             pltpu.VMEM((n_mz, part, cols), f32),
@@ -510,7 +497,6 @@
             dma((chunks,)),
             dma((away, chunks)),
             dma((away, chunks)),
-            dma((ring,)),
             dma((kept,)),
             dma((kept,)),
             dma((1,)),
@@ -524,7 +510,7 @@
             bytes_accessed=2 * bins * (rows + cols + share),
             transcendentals=0,
         ),
-    )(spectra, u, probes)
+    )(spectra, kernel, probes)
 
 
 def solution(mesh):

time: 139 us -> 133 us (0.957)
  local copies, waits for them, and re-layouts: 6.67 us -> 2.63 us
  Pallas kernels: 131 us -> 129 us
    unnamed x4 -> x2, local copies, waits for them, and re-layouts: 6.67 us -> 2.63 us
    pallas_call x1, Pallas kernels: 131 us -> 129 us  [per_device(): pl.pallas_call(functools.partial(fused_kernel, n_mz, n_pix, factor, float...]
where the time goes in v1:
time: 133 us; the launch traced here: 132 us
  Pallas kernels  129 us (97%)
  local copies, waits for them, and re-layouts  2.63 us (2%)
    pallas_call x1, Pallas kernels, per_device(): pl.pallas_call(functools.partial(fused_kernel, n_mz, n_pix, factor, float...  129 us

profile of v1, /device:TPU:0, one launch (start us, length us, event | category | flops | bytes accessed | tf_op | source)
XLA Modules:
  0.0 132.4 jit_solution(353280247905704363)
XLA Ops:
  0.6 129.1 %shard_map.50 = (bf16[128,128]{1,0:T(8,128)(2,1)S(1)}, bf16[32,65536]{1,0:T(8,128)(2,1)S(1)}) custom-call(bf16[128,65536]{1,0:T(8,128)(2,1)} %spectra.1, bf16[129]{0:T(256)(128)(2,1)} %k_ref.1, bf16[65536,128]{1,0:T(8,128)(2,1)} %probes.1), custom_call_target="tpu_custom_call" | custom-call | flops 12884901888 | bytes 37748736 | tf_op jit(solution)/shard_map/pallas_call | solution.py:450
  129.7 0.6 copy.7
  130.3 2.0 %copy.8 = bf16[32,65536]{1,0:T(8,128)(2,1)} copy(bf16[32,65536]{1,0:T(8,128)(2,1)S(1)} %get-tuple-element.3) | data formatting | bytes 8388608

commit v2 on v1

--- a/solution.py
+++ b/solution.py
@@ -16,8 +16,9 @@
 MESH = pl.DeviceIdType.MESH
 HIGHEST = lax.Precision.HIGHEST
 PANEL = 8
-EARLY = 5
-AHEAD = 4
+EARLY = 4
+PIECES = 4
+MARKS = (12, 13, 13, 16)
 MET = 4
 
 
@@ -60,9 +61,20 @@
                     x[later] = x[later] - scale * rows_q[t]
 
 
+def write_kernel(basis, projected, basis_out, projected_out, sem):
+    copies = [
+        pltpu.make_async_copy(projected, projected_out, sem.at[0]),
+        pltpu.make_async_copy(basis, basis_out, sem.at[1]),
+    ]
+    for copy in copies:
+        copy.start()
+    for copy in copies:
+        copy.wait()
+
+
 def fused_kernel(
-    n_mz, n_pix, factor, pixels, early, ahead, spectra, k_ref, probes, basis, out,
-    raw, tap, line, w_ref, halo, cleaned, total, parts, parts_in, sketch, gram, gram_in, x_ref,
+    n_mz, n_pix, factor, pixels, early, marks, spectra, k_ref, probes, basis, out,
+    raw, tap, line, w_ref, edge_ref, halo, cleaned, total, parts, parts_in, sketch, gram, gram_sum, gram_in, x_ref,
     lhs, give, core_in, hold, x_give, x_in, acc, lhs_far, early_in, sketch_far,
     raw_sem, tap_sem, halo_send, halo_recv, parts_send, parts_recv, all_send, all_recv,
     gram_send, gram_recv, give_sem, core_sem, x_send_sem, x_recv_sem,
@@ -131,12 +143,20 @@
         return jnp.where(i < per, i, jnp.where(
             i < both, i + 2 * early, whole_of(i - both, chip)))
 
-    def send_early(e):
+    def send_early(i):
+        e, piece = i // PIECES, i % PIECES
+        size = early_in.shape[1] // PIECES
+        at = pl.ds(piece * size, size)
         return pltpu.make_async_remote_copy(
-            src_ref=cleaned.at[whole_of(e, 1 - chip)], dst_ref=early_in.at[e],
-            send_sem=early_send.at[e], recv_sem=early_recv.at[e],
+            src_ref=cleaned.at[whole_of(e, 1 - chip), at], dst_ref=early_in.at[e, at],
+            send_sem=early_send.at[i], recv_sem=early_recv.at[i],
             device_id=device(1 - chip, core), device_id_type=MESH,
         )
+
+    def start_early(step):
+        low, high = ((0,) + marks)[step : step + 2]
+        for i in range(low, high):
+            send_early(i).start()
 
     for pos in range(min(slots, tiles)):
         each_load(jnp.int32(pos), lambda c: c.start())
@@ -152,7 +172,13 @@
     line[:, :taps] = k_ref[...].astype(jnp.float32).reshape(1, taps)
     base = jnp.broadcast_to(line[...], (OUT, WIN))
     band = pltpu.roll(base, LANES - taps // 2, 1, stride=1, stride_axis=0)
-    w_ref[...] = band.T.astype(jnp.bfloat16)
+    full_band = band.T.astype(jnp.bfloat16)
+    w_ref[...] = full_band[LANES : LANES + OUT]
+    low = lax.broadcasted_iota(jnp.int32, (LANES, LANES), 0) < LANES // 2
+    corner = jnp.where(low, full_band[WIN - LANES :, OUT - LANES :], full_band[:LANES, :LANES])
+    edge_ref[...] = jnp.zeros_like(edge_ref)
+    edge_ref[:LANES, :LANES] = corner
+    edge_ref[LANES:, LANES:] = corner
     total[...] = jnp.zeros_like(total)
 
     to_right = pltpu.make_async_remote_copy(
@@ -195,19 +221,44 @@
 
             raw[slot, :, tile + LANES :] = halo[1]
 
-        w = w_ref[...]
-        done = []
-        for j in range(tile // OUT):
-            window = raw[slot, :, j * OUT : j * OUT + WIN]
-            smooth = jnp.dot(window, w, preferred_element_type=jnp.float32)
-            mine = raw[slot, :, LANES + j * OUT : LANES + (j + 1) * OUT].astype(jnp.float32)
-            one = (mine - smooth).astype(jnp.bfloat16)
-            piece, inside = (j * OUT) // width, (j * OUT) % width
-            cleaned[at * per + piece, :, inside : inside + OUT] = one
-            done.append(one)
-        total[...] += jnp.dot(
-            jnp.concatenate(done, axis=1), tap[slot], preferred_element_type=jnp.float32
-        )
+        w, edge = w_ref[...], edge_ref[...]
+        low = lax.broadcasted_iota(jnp.int32, (raw.shape[1], LANES), 1) < LANES // 2
+        block = lambda i: raw[slot, :, LANES + i * LANES : LANES + (i + 1) * LANES]
+        group = min(4, width // OUT)
+        ready, added = [], None
+
+        def sketch_part(js, added):
+            begin, end = js[0] * OUT, (js[-1] + 1) * OUT
+            piece, inside = begin // width, begin % width
+            one = jnp.dot(
+                cleaned[at * per + piece, :, inside : inside + end - begin],
+                tap[slot, begin:end], preferred_element_type=jnp.float32,
+            )
+            return one if added is None else added + one
+
+        for j in range(0, tile // OUT, 2):
+            sides = [jnp.where(low, block(2 * k + 2), block(2 * k - 1)) for k in (j, j + 1)]
+            outer = jnp.dot(
+                jnp.concatenate(sides, axis=1), edge, preferred_element_type=jnp.float32
+            )
+            for k in (j, j + 1):
+                mine = raw[slot, :, LANES + k * OUT : LANES + (k + 1) * OUT]
+                inner = jnp.dot(mine, w, preferred_element_type=jnp.float32)
+                side = outer[:, (k - j) * LANES : (k - j + 1) * LANES]
+                smooth = inner + jnp.concatenate(
+                    [jnp.where(low, side, 0.0), jnp.where(low, 0.0, side)], axis=1
+                )
+                one = (mine.astype(jnp.float32) - smooth).astype(jnp.bfloat16)
+                piece, inside = (k * OUT) // width, (k * OUT) % width
+                cleaned[at * per + piece, :, inside : inside + OUT] = one
+            ready += [j, j + 1]
+            if len(ready) >= 2 * group:
+                added = sketch_part(ready[:group], added)
+                ready = ready[group:]
+        while ready:
+            added = sketch_part(ready[:group], added)
+            ready = ready[group:]
+        total[...] += added
 
     @pl.loop(0, tiles)
     def _(pos):
@@ -223,8 +274,7 @@
             def _():
                 to_left.start()
 
-            for e in range(ahead):
-                send_early(e).start()
+            start_early(0)
 
         clean(pos)
 
@@ -253,6 +303,7 @@
 
     for d in range(1, n_mz):
         scatter(d).start()
+    start_early(1)
     mine = parts[mz]
     for d in range(1, n_mz):
         scatter(d).wait_recv()
@@ -268,6 +319,7 @@
 
     for d in range(1, n_mz):
         gather(d, mz).start()
+    start_early(2)
     for d in range(1, n_mz):
         gather(d, lax.rem(mz + n_mz - d, n_mz)).wait_recv()
     sk = jnp.concatenate([sketch[z] for z in range(n_mz)], axis=0)
@@ -280,10 +332,16 @@
         return pltpu.make_async_remote_copy(
             src_ref=gram, dst_ref=gram_in.at[d - 1],
             send_sem=gram_send.at[d - 1], recv_sem=gram_recv.at[d - 1],
-            device_id=at_pix(d), device_id_type=MESH,
+            device_id=device(chip_of(d), core), device_id_type=MESH,
         )
 
-    for d in range(1, n_pix):
+    relay = pltpu.make_async_remote_copy(
+        src_ref=gram_sum, dst_ref=gram_in.at[chips - 1],
+        send_sem=gram_send.at[chips - 1], recv_sem=gram_recv.at[chips - 1],
+        device_id=device(chip, other), device_id_type=MESH,
+    )
+
+    for d in range(1, chips):
         share_gram(d).start()
     to_far = pltpu.make_async_remote_copy(
         src_ref=sketch, dst_ref=sketch_far, send_sem=far_send.at[0], recv_sem=far_recv.at[0],
@@ -292,13 +350,16 @@
     if early:
         to_far.start()
     full = gram[...]
-    for d in range(1, n_pix):
+    for d in range(1, chips):
         share_gram(d).wait_recv()
         full = full + gram_in[d - 1]
+    gram_sum[...] = full
+    relay.start()
+    relay.wait_recv()
+    full = full + gram_in[chips - 1]
     if early:
         to_far.wait_recv()
-        for e in range(ahead, early):
-            send_early(e).start()
+        start_early(3)
     total[...] = full * (1.0 / pixels)
     whiten(total, x_ref)
     x = x_ref[...]
@@ -343,7 +404,8 @@
 
         part = product(lhs[...], cleaned[chunk_of(i)])
         if alone:
-            send_early(i - both).wait_recv()
+            for piece in range(PIECES):
+                send_early((i - both) * PIECES + piece).wait_recv()
             far = product(lhs_far[...], early_in[i - both])
             part = (part.astype(jnp.float32) + far.astype(jnp.float32)).astype(jnp.bfloat16)
         give[slot] = part[:half]
@@ -398,12 +460,13 @@
     for d in range(1, n_mz):
         scatter(d).wait_send()
         gather(d, mz).wait_send()
-    for d in range(1, n_pix):
+    for d in range(1, chips):
         share_gram(d).wait_send()
+    relay.wait_send()
     if early:
         to_far.wait_send()
-        for e in range(early):
-            send_early(e).wait_send()
+        for i in range(early * PIECES):
+            send_early(i).wait_send()
 
         @pl.loop(0, early)
         def _(e):
@@ -441,14 +504,14 @@
     chunks = bins // width
     slots, ring = 3, 4
     fits = chips == 2 and tile % width == 0 and bins // tile >= 8
-    early, ahead = (EARLY, AHEAD) if fits else (0, 0)
+    early, marks = (EARLY, MARKS) if fits else (0, (0, 0, 0, 0))
     kept = max(early, 1)
     away = max(chips - 1, 1)
     part = rows // n_mz
     bf16, f32 = jnp.bfloat16, jnp.float32
     dma = pltpu.SemaphoreType.DMA
-    return pl.pallas_call(
-        functools.partial(fused_kernel, n_mz, n_pix, factor, float(pixels), early, ahead),
+    held = pl.pallas_call(
+        functools.partial(fused_kernel, n_mz, n_pix, factor, float(pixels), early, marks),
         in_specs=[
             pl.BlockSpec(memory_space=pl.ANY),
             pl.BlockSpec(memory_space=pltpu.VMEM),
@@ -463,7 +526,8 @@
             pltpu.VMEM((slots, rows, tile + 2 * LANES), bf16),
             pltpu.VMEM((slots, tile, cols), bf16),
             pltpu.VMEM((1, WIN), f32),
-            pltpu.VMEM((WIN, OUT), bf16),
+            pltpu.VMEM((OUT, OUT), bf16),
+            pltpu.VMEM((OUT, OUT), bf16),
             pltpu.VMEM((2, rows, LANES), bf16),
             pltpu.VMEM((chunks, rows, width), bf16),
             pltpu.VMEM((rows, cols), f32),
@@ -471,7 +535,8 @@
             pltpu.VMEM((n_mz - 1, part, cols), f32),
             pltpu.VMEM((n_mz, part, cols), f32),
             pltpu.VMEM((cols, cols), f32),
-            pltpu.VMEM((n_pix - 1, cols, cols), f32),
+            pltpu.VMEM((cols, cols), f32),
+            pltpu.VMEM((chips, cols, cols), f32),
             pltpu.VMEM((cols, cols), f32),
             pltpu.VMEM((cols, rows), bf16),
             pltpu.VMEM((ring, half, width), bf16),
@@ -491,14 +556,14 @@
             dma((n_mz - 1,)),
             dma((n_mz - 1,)),
             dma((n_mz - 1,)),
-            dma((n_pix - 1,)),
-            dma((n_pix - 1,)),
+            dma((chips,)),
+            dma((chips,)),
             dma((ring,)),
             dma((chunks,)),
             dma((away, chunks)),
             dma((away, chunks)),
-            dma((kept,)),
-            dma((kept,)),
+            dma((kept * PIECES,)),
+            dma((kept * PIECES,)),
             dma((1,)),
             dma((1,)),
         ],
@@ -511,6 +576,17 @@
             transcendentals=0,
         ),
     )(spectra, kernel, probes)
+    return pl.pallas_call(
+        write_kernel,
+        in_specs=[pl.BlockSpec(memory_space=pltpu.VMEM)] * 2,
+        out_specs=[pl.BlockSpec(memory_space=pl.ANY)] * 2,
+        out_shape=[
+            jax.ShapeDtypeStruct((rows, cols), bf16),
+            jax.ShapeDtypeStruct((share, bins), bf16),
+        ],
+        scratch_shapes=[dma((2,))],
+        compiler_params=pltpu.CompilerParams(vmem_limit_bytes=2**20),
+    )(*[pltpu.with_memory_space_constraint(one, pltpu.VMEM) for one in held])
 
 
 def solution(mesh):

time: 133 us -> 129 us (0.970)
  local copies, waits for them, and re-layouts: 2.63 us -> 0 us
    pallas_call x1, Pallas kernels: 129 us -> 126 us  [per_device(): pl.pallas_call(functools.partial(fused_kernel, n_mz, n_pix, factor, float...]
    unnamed x2 -> x0, local copies, waits for them, and re-layouts: 2.63 us -> none
    pallas_call x0 -> x1, Pallas kernels: none -> 2.03 us  [per_device(): pl.pallas_call(write_kernel, in_specs=[pl.BlockSpec(memory_space=pltpu.VM...]
where the time goes in v2:
time: 129 us
  Pallas kernels  128 us (99%)
    pallas_call x1, Pallas kernels, per_device(): pl.pallas_call(functools.partial(fused_kernel, n_mz, n_pix, factor, float...  126 us

profile of v2, /device:TPU:0, one launch (start us, length us, event | category | flops | bytes accessed | tf_op | source)
XLA Modules:
  0.0 129.0 jit_solution(4994801148804087387)
XLA Ops:
  0.6 126.3 %shard_map.50 = (bf16[128,128]{1,0:T(8,128)(2,1)S(1)}, bf16[32,65536]{1,0:T(8,128)(2,1)S(1)}) custom-call(bf16[128,65536]{1,0:T(8,128)(2,1)} %spectra.1, bf16[129]{0:T(256)(128)(2,1)} %k_ref.1, bf16[65536,128]{1,0:T(8,128)(2,1)} %probes.1), custom_call_target="tpu_custom_call" | custom-call | flops 12884901888 | bytes 37748736 | tf_op jit(solution)/shard_map/pallas_call | solution.py:513
  126.9 2.0 %shard_map.51 = (bf16[128,128]{1,0:T(8,128)(2,1)}, bf16[32,65536]{1,0:T(8,128)(2,1)}) custom-call(bf16[128,128]{1,0:T(8,128)(2,1)S(1)} %get-tuple-element.4.basis, bf16[32,65536]{1,0:T(8,128)(2,1)S(1)} %get-tuple-element.5.projected), custom_call_target="tpu_custom_call" | custom-call | tf_op jit(solution)/shard_map/pallas_call | solution.py:579

commit v3 on v2

--- a/solution.py
+++ b/solution.py
@@ -15,50 +15,67 @@
 
 MESH = pl.DeviceIdType.MESH
 HIGHEST = lax.Precision.HIGHEST
-PANEL = 8
+PANEL = 16
+PANELS = 4
 EARLY = 4
 PIECES = 4
-MARKS = (12, 13, 13, 16)
+MARKS = (13, 14, 14, 16)
 MET = 4
 
 
 def whiten(a_ref, x_ref):
     size = a_ref.shape[0]
+    blocks = size // PANEL
     row = lax.broadcasted_iota(jnp.int32, (PANEL, 1), 0)
     a = a_ref[...]
     x = (
         lax.broadcasted_iota(jnp.int32, (size, size), 0)
         == lax.broadcasted_iota(jnp.int32, (size, size), 1)
     ).astype(jnp.float32)
-    blocks = size // PANEL
     a = [a[i * PANEL : (i + 1) * PANEL] for i in range(blocks)]
     x = [x[i * PANEL : (i + 1) * PANEL] for i in range(blocks)]
     for index in range(blocks):
-        p, q = a[index], x[index]
-        rows_p, rows_q = [], []
-        spread = [
-            jnp.broadcast_to(p[:, index * PANEL + t : index * PANEL + t + 1], p.shape)
-            for t in range(PANEL)
-        ]
+        base = index * PANEL
+        first = index - index % PANELS
+        last = min(first + PANELS, blocks)
+        rows_a, rows_x = [], []
+        spread = {
+            i: [
+                jnp.broadcast_to(a[i][:, base + t : base + t + 1], (PANEL, size))
+                for t in range(PANEL)
+            ]
+            for i in range(index, last)
+        }
+        own = spread[index]
         for t in range(PANEL):
-            inv = lax.rsqrt(spread[t][t : t + 1])
-            r, y = p[t : t + 1] * inv, q[t : t + 1] * inv
-            rows_p.append(r)
-            rows_q.append(y)
-            if t + 1 < PANEL:
-                scale = jnp.where(row > t, spread[t] * inv, 0.0)
-                p = p - scale * r
-                q = q - scale * y
+            inv = lax.rsqrt(own[t][t : t + 1])
+            across = [own[j][t : t + 1] * inv for j in range(t + 1, PANEL)]
+            r, y = a[index][t : t + 1] * inv, x[index][t : t + 1] * inv
+            rows_a.append(r)
+            rows_x.append(y)
+            for i in range(index, last):
+                scale = spread[i][t] * inv
+                if i == index:
+                    if t + 1 == PANEL:
+                        continue
+                    scale = jnp.where(row > t, scale, 0.0)
                 for j in range(t + 1, PANEL):
-                    spread[j] = spread[j] - scale * (spread[j][t : t + 1] * inv)
-        x_ref[index * PANEL : (index + 1) * PANEL, :] = jnp.concatenate(rows_q, axis=0)
-        if index + 1 < blocks:
-            turned = jnp.concatenate(rows_p, axis=0).T
-            for later in range(index + 1, blocks):
-                for t in range(PANEL):
-                    scale = turned[later * PANEL : (later + 1) * PANEL, t : t + 1]
-                    a[later] = a[later] - scale * rows_p[t]
-                    x[later] = x[later] - scale * rows_q[t]
+                    spread[i][j] = spread[i][j] - scale * across[j - t - 1]
+                a[i] = a[i] - scale * r
+                x[i] = x[i] - scale * y
+        a[index], x[index] = jnp.concatenate(rows_a, axis=0), jnp.concatenate(rows_x, axis=0)
+        x_ref[base : base + PANEL, :] = x[index]
+        if index + 1 == last and last < blocks:
+            done = jnp.concatenate(a[first:last], axis=0)
+            both = jnp.concatenate([done, jnp.concatenate(x[first:last], axis=0)], axis=1)
+            minus = lax.dot_general(
+                done, both, (((0,), (0,)), ((), ())), precision=HIGHEST,
+                preferred_element_type=jnp.float32,
+            )
+            for later in range(last, blocks):
+                rows = minus[later * PANEL : (later + 1) * PANEL]
+                a[later] = a[later] - rows[:, :size]
+                x[later] = x[later] - rows[:, size:]
 
 
 def write_kernel(basis, projected, basis_out, projected_out, sem):
@@ -75,7 +92,7 @@
 def fused_kernel(
     n_mz, n_pix, factor, pixels, early, marks, spectra, k_ref, probes, basis, out,
     raw, tap, line, w_ref, edge_ref, halo, cleaned, total, parts, parts_in, sketch, gram, gram_sum, gram_in, x_ref,
-    lhs, give, core_in, hold, x_give, x_in, acc, lhs_far, early_in, sketch_far,
+    lhs, give, core_in, hold, x_give, x_in, acc, lhs_far, early_in, flat, flat_far,
     raw_sem, tap_sem, halo_send, halo_recv, parts_send, parts_recv, all_send, all_recv,
     gram_send, gram_recv, give_sem, core_sem, x_send_sem, x_recv_sem,
     early_send, early_recv, far_send, far_recv,
@@ -158,8 +175,7 @@
         for i in range(low, high):
             send_early(i).start()
 
-    for pos in range(min(slots, tiles)):
-        each_load(jnp.int32(pos), lambda c: c.start())
+    each_load(jnp.int32(0), lambda c: c.start())
 
     barrier = pltpu.get_barrier_semaphore()
     for d in range(1, n_mz):
@@ -180,6 +196,8 @@
     edge_ref[:LANES, :LANES] = corner
     edge_ref[LANES:, LANES:] = corner
     total[...] = jnp.zeros_like(total)
+    for pos in range(1, min(slots, tiles)):
+        each_load(jnp.int32(pos), lambda c: c.start())
 
     to_right = pltpu.make_async_remote_copy(
         src_ref=spectra.at[:, pl.ds(bins - LANES, LANES)], dst_ref=halo.at[0],
@@ -224,15 +242,19 @@
         w, edge = w_ref[...], edge_ref[...]
         low = lax.broadcasted_iota(jnp.int32, (raw.shape[1], LANES), 1) < LANES // 2
         block = lambda i: raw[slot, :, LANES + i * LANES : LANES + (i + 1) * LANES]
-        group = min(4, width // OUT)
+        group = 4
         ready, added = [], None
 
         def sketch_part(js, added):
             begin, end = js[0] * OUT, (js[-1] + 1) * OUT
-            piece, inside = begin // width, begin % width
+            step = min(width, end - begin)
+            pieces = [
+                cleaned[at * per + i // width, :, i % width : i % width + step]
+                for i in range(begin, end, step)
+            ]
             one = jnp.dot(
-                cleaned[at * per + piece, :, inside : inside + end - begin],
-                tap[slot, begin:end], preferred_element_type=jnp.float32,
+                jnp.concatenate(pieces, axis=1), tap[slot, begin:end],
+                preferred_element_type=jnp.float32,
             )
             return one if added is None else added + one
 
@@ -324,8 +346,15 @@
         gather(d, lax.rem(mz + n_mz - d, n_mz)).wait_recv()
     sk = jnp.concatenate([sketch[z] for z in range(n_mz)], axis=0)
 
-    gram[...] = lax.dot_general(
+    square = lax.dot_general(
         sk, sk, (((0,), (0,)), ((), ())), precision=HIGHEST, preferred_element_type=jnp.float32
+    )
+    size = square.shape[0]
+    top, strip = size // 2, size // 4
+    gram[:top] = square[:top]
+    left = lax.broadcasted_iota(jnp.int32, (strip, size), 1) < top
+    gram[top:] = jnp.where(
+        left, pltpu.roll(square[top : top + strip], top, 1), square[top + strip :]
     )
 
     def share_gram(d):
@@ -344,11 +373,9 @@
     for d in range(1, chips):
         share_gram(d).start()
     to_far = pltpu.make_async_remote_copy(
-        src_ref=sketch, dst_ref=sketch_far, send_sem=far_send.at[0], recv_sem=far_recv.at[0],
+        src_ref=flat, dst_ref=flat_far, send_sem=far_send.at[0], recv_sem=far_recv.at[0],
         device_id=device(1 - chip, core), device_id_type=MESH,
     )
-    if early:
-        to_far.start()
     full = gram[...]
     for d in range(1, chips):
         share_gram(d).wait_recv()
@@ -358,24 +385,28 @@
     relay.wait_recv()
     full = full + gram_in[chips - 1]
     if early:
-        to_far.wait_recv()
         start_early(3)
-    total[...] = full * (1.0 / pixels)
+    full = full * (1.0 / pixels)
+    total[:top] = full[:top]
+    total[top : top + strip] = pltpu.roll(full[top:], top, 1)
+    total[top + strip :] = full[top:]
     whiten(total, x_ref)
     x = x_ref[...]
     by_lane = (((1,), (1,)), ((), ()))
 
-    def fill(target, of):
-        flipped = lax.dot_general(
-            x, of, by_lane, precision=HIGHEST, preferred_element_type=jnp.float32
-        ).astype(jnp.bfloat16)
-        basis_t = flipped.reshape(n_pix, share, flipped.shape[1])
+    def fill(target, source):
+        basis_t = source[...].reshape(n_pix, share, source.shape[1])
         for chunk in range(n_pix):
             d = lax.rem(chunk // 2 - chip + chips, chips)
             at = d * share + jnp.where(core == chunk % 2, half, 0)
             target[pl.ds(pl.multiple_of(at, share), share), :] = basis_t[chunk]
 
-    fill(lhs, sk)
+    flat[...] = lax.dot_general(
+        x, sk, by_lane, precision=HIGHEST, preferred_element_type=jnp.float32
+    ).astype(jnp.bfloat16)
+    if early:
+        to_far.start()
+    fill(lhs, flat)
 
     def to_core(k):
         return pltpu.make_async_remote_copy(
@@ -432,17 +463,18 @@
     def _(i):
         first(i, False)
 
-    basis[...] = lax.dot_general(
-        sk, x, by_lane, precision=HIGHEST, preferred_element_type=jnp.float32
-    ).astype(jnp.bfloat16)
-
     @pl.loop(lag, both)
     def _(i):
         first(i, False)
         second(i - lag)
 
+    basis[...] = lax.dot_general(
+        sk, x, by_lane, precision=HIGHEST, preferred_element_type=jnp.float32
+    ).astype(jnp.bfloat16)
+
     if early:
-        fill(lhs_far, jnp.concatenate([sketch_far[z] for z in range(n_mz)], axis=0))
+        to_far.wait_recv()
+        fill(lhs_far, flat_far)
 
         @pl.loop(both, mine)
         def _(i):
@@ -534,9 +566,9 @@
             pltpu.VMEM((n_mz, part, cols), f32),
             pltpu.VMEM((n_mz - 1, part, cols), f32),
             pltpu.VMEM((n_mz, part, cols), f32),
-            pltpu.VMEM((cols, cols), f32),
-            pltpu.VMEM((cols, cols), f32),
-            pltpu.VMEM((chips, cols, cols), f32),
+            pltpu.VMEM((cols // 4 * 3, cols), f32),
+            pltpu.VMEM((cols // 4 * 3, cols), f32),
+            pltpu.VMEM((chips, cols // 4 * 3, cols), f32),
             pltpu.VMEM((cols, cols), f32),
             pltpu.VMEM((cols, rows), bf16),
             pltpu.VMEM((ring, half, width), bf16),
@@ -547,7 +579,8 @@
             pltpu.VMEM((chunks, share, width), f32),
             pltpu.VMEM((cols, rows), bf16),
             pltpu.VMEM((kept, rows, width), bf16),
-            pltpu.VMEM((n_mz, part, cols), f32),
+            pltpu.VMEM((cols, rows), bf16),
+            pltpu.VMEM((cols, rows), bf16),
             dma((slots,)),
             dma((slots,)),
             dma((2,)),

time: 129 us -> 127 us (0.984)
  Pallas kernels: 128 us -> 126 us
    pallas_call x1, Pallas kernels: 126 us -> 124 us  [per_device(): pl.pallas_call(functools.partial(fused_kernel, n_mz, n_pix, factor, float...]
where the time goes in v3:
time: 127 us
  Pallas kernels  126 us (99%)
    pallas_call x1, Pallas kernels, per_device(): pl.pallas_call(functools.partial(fused_kernel, n_mz, n_pix, factor, float...  124 us

profile of v3, /device:TPU:0, one launch (start us, length us, event | category | flops | bytes accessed | tf_op | source)
XLA Modules:
  0.0 126.6 jit_solution(17886378544710218558)
XLA Ops:
  0.6 123.9 %shard_map.50 = (bf16[128,128]{1,0:T(8,128)(2,1)S(1)}, bf16[32,65536]{1,0:T(8,128)(2,1)S(1)}) custom-call(bf16[128,65536]{1,0:T(8,128)(2,1)} %spectra.1, bf16[129]{0:T(256)(128)(2,1)} %k_ref.1, bf16[65536,128]{1,0:T(8,128)(2,1)} %probes.1), custom_call_target="tpu_custom_call" | custom-call | flops 12884901888 | bytes 37748736 | tf_op jit(solution)/shard_map/pallas_call | solution.py:545
  124.5 2.0 %shard_map.51 = (bf16[128,128]{1,0:T(8,128)(2,1)}, bf16[32,65536]{1,0:T(8,128)(2,1)}) custom-call(bf16[128,128]{1,0:T(8,128)(2,1)S(1)} %get-tuple-element.4.basis, bf16[32,65536]{1,0:T(8,128)(2,1)S(1)} %get-tuple-element.5.projected), custom_call_target="tpu_custom_call" | custom-call | tf_op jit(solution)/shard_map/pallas_call | solution.py:612

commit v4 on v3

--- a/solution.py
+++ b/solution.py
@@ -17,8 +17,9 @@
 HIGHEST = lax.Precision.HIGHEST
 PANEL = 16
 PANELS = 4
-EARLY = 4
-PIECES = 4
+EARLY = 2
+LAG = 1
+PIECES = 8
 MARKS = (13, 14, 14, 16)
 MET = 4
 
@@ -456,7 +457,7 @@
     def emit(k, value):
         out[:, pl.ds(pl.multiple_of(k * width, width), width)] = value.astype(jnp.bfloat16)
 
-    lag = min(ring - 1, both)
+    lag = min(LAG, ring - 1, both)
     mine = chunks - early
 
     @pl.loop(0, lag)
@@ -532,7 +533,7 @@
     chips = n_pix // 2
     half = chips * share
     tile = min(4096, bins // 2)
-    width = min(1024, tile)
+    width = min(2048, tile)
     chunks = bins // width
     slots, ring = 3, 4
     fits = chips == 2 and tile % width == 0 and bins // tile >= 8

time: 127 us -> 126 us (level)
  no operation moved by 1% of the time
where the time goes in v4:
time: 126 us
  Pallas kernels  125 us (99%)
    pallas_call x1, Pallas kernels, per_device(): pl.pallas_call(functools.partial(fused_kernel, n_mz, n_pix, factor, float...  123 us

profile of v4, /device:TPU:0, one launch (start us, length us, event | category | flops | bytes accessed | tf_op | source)
XLA Modules:
  0.0 125.5 jit_solution(7222702876865152890)
XLA Ops:
  0.6 122.9 %shard_map.50 = (bf16[128,128]{1,0:T(8,128)(2,1)S(1)}, bf16[32,65536]{1,0:T(8,128)(2,1)S(1)}) custom-call(bf16[128,65536]{1,0:T(8,128)(2,1)} %spectra.1, bf16[129]{0:T(256)(128)(2,1)} %k_ref.1, bf16[65536,128]{1,0:T(8,128)(2,1)} %probes.1), custom_call_target="tpu_custom_call" | custom-call | flops 12884901888 | bytes 37748736 | tf_op jit(solution)/shard_map/pallas_call | solution.py:546
  123.5 2.0 %shard_map.51 = (bf16[128,128]{1,0:T(8,128)(2,1)}, bf16[32,65536]{1,0:T(8,128)(2,1)}) custom-call(bf16[128,128]{1,0:T(8,128)(2,1)S(1)} %get-tuple-element.4.basis, bf16[32,65536]{1,0:T(8,128)(2,1)S(1)} %get-tuple-element.5.projected), custom_call_target="tpu_custom_call" | custom-call | tf_op jit(solution)/shard_map/pallas_call | solution.py:613

commit v5 on v4

--- a/solution.py
+++ b/solution.py
@@ -19,8 +19,8 @@
 PANELS = 4
 EARLY = 2
 LAG = 1
-PIECES = 8
-MARKS = (13, 14, 14, 16)
+PIECES = 4
+MARKS = (7, 7, 7, 8)
 MET = 4
 
 

time: 126 us -> 126 us (level)
  no operation moved by 1% of the time
where the time goes in v5:
time: 126 us; the launch traced here: 125 us
  Pallas kernels  125 us (99%)
    pallas_call x1, Pallas kernels, per_device(): pl.pallas_call(functools.partial(fused_kernel, n_mz, n_pix, factor, float...  123 us

profile of v5, /device:TPU:0, one launch (start us, length us, event | category | flops | bytes accessed | tf_op | source)
XLA Modules:
  0.0 125.3 jit_solution(15718639761123025601)
XLA Ops:
  0.6 122.7 %shard_map.50 = (bf16[128,128]{1,0:T(8,128)(2,1)S(1)}, bf16[32,65536]{1,0:T(8,128)(2,1)S(1)}) custom-call(bf16[128,65536]{1,0:T(8,128)(2,1)} %spectra.1, bf16[129]{0:T(256)(128)(2,1)} %k_ref.1, bf16[65536,128]{1,0:T(8,128)(2,1)} %probes.1), custom_call_target="tpu_custom_call" | custom-call | flops 12884901888 | bytes 37748736 | tf_op jit(solution)/shard_map/pallas_call | solution.py:546
  123.3 2.0 %shard_map.51 = (bf16[128,128]{1,0:T(8,128)(2,1)}, bf16[32,65536]{1,0:T(8,128)(2,1)}) custom-call(bf16[128,128]{1,0:T(8,128)(2,1)S(1)} %get-tuple-element.4.basis, bf16[32,65536]{1,0:T(8,128)(2,1)S(1)} %get-tuple-element.5.projected), custom_call_target="tpu_custom_call" | custom-call | tf_op jit(solution)/shard_map/pallas_call | solution.py:613
